TPU v7x, 32 devices: a whole 2x2x4 slice. The times are simulated.
32 devices in a mesh: segment: 2 (over x), tensor: 16 (over z, y, core).
Axes of the slice: x: 2, y: 2, z: 4, core: 2. Of those that a mesh axis runs over, the one named last changes fastest.
Arguments:
- step_inputs: bfloat16 [3, 16, 8192], P(None, None, 'tensor'), may hold values from -6 to 6
- norm_gain: float32 [2, 8192], P('segment'), may hold values from 0.1 to 1.9
- query_weight: bfloat16 [2, 8192, 8192], P('segment', None, 'tensor'), may hold values from -0.0625 to 0.0625
- kv_weight: bfloat16 [2, 8192, 2, 1024], P('segment', None, None, 'tensor'), may hold values from -0.125 to 0.125
- out_weight: bfloat16 [2, 8192, 8192], P('segment', None, 'tensor'), may hold values from -0.125 to 0.125
- kv_cache: bfloat16 [2, 16, 3, 128, 256], P('segment', 'tensor'), as said below
- block_table: int32 [16, 2], replicated, may hold values from 0 to 2, as said below
- prefix_len: int32 [16], replicated, may hold values from 1 to 256, as said below
- parents: int32 [3, 16], replicated, may hold values from 0 to 15
Outputs:
- received: bfloat16 [2, 3, 16, 8192], P('segment', None, None, 'tensor')
Inputs may be any that keep to these rules, and one draw needn't show every extreme that they name: `block_table`: every row of one source has the same first entry; its second entry is one of two blocks of that source, each of them used by some row; no block serves two sources. `prefix_len`: some row holds 256 tokens. `kv_cache`: copies c and c' are equal when c * 64 // (number of copies) // 8 equals the same for c'.
All inputs are finite; a program needn't handle non-finite values.
Results may differ from a plain program's by a relative error of at most 0.012.
The roundings to bfloat16 on the way count: a program that leaves them out, or rounds other values in their place, can miss the bound.
Values may be sent and summed in bfloat16 or wider, within the bound.
A program may use at most 64 MiB of HBM per device.

v0:
```python
import jax
import jax.numpy as jnp
from jax import lax
from jax.sharding import PartitionSpec as P

KV_HEADS = 8
HEAD_SIZE = 128
BEAMS = 16
BLOCK = 128
STEPS = 3
SOURCES = 1
GROUP = 8
ROPE_BASE = 1000000.0
NORM_EPS = 1e-06
MASK_FLOOR = -1e30


def shifted(block, axis, distance):
    devices = range(lax.axis_size(axis))
    route = [((i - distance) % len(devices), i) for i in devices]
    return lax.ppermute(block, axis, route)


def normalize(rows_in, gain):
    widened = rows_in.astype(jnp.float32)
    mean_square = jnp.mean(widened * widened, axis=-1, keepdims=True)
    return (widened * lax.rsqrt(mean_square + NORM_EPS) * gain).astype(jnp.bfloat16)


def rotate(values, positions):
    half_size = values.shape[-1] // 2
    exponent = jnp.arange(half_size, dtype=jnp.float32) * (2.0 / values.shape[-1])
    frequency = jnp.power(jnp.float32(ROPE_BASE), -exponent)
    angles = positions.astype(jnp.float32)[:, None] * frequency[None, :]
    angles = jnp.concatenate([angles, angles], axis=-1)[:, None, :]
    front_part = values[..., :half_size]
    back_part = values[..., half_size:]
    turned = jnp.concatenate([-back_part, front_part], axis=-1)
    return values * jnp.cos(angles) + turned * jnp.sin(angles)


def ancestry(parents):
    rows_all = parents.shape[1]
    source_start = jnp.arange(rows_all, dtype=jnp.int32) // BEAMS * BEAMS
    lineage = []
    root_table = []
    for later_step in range(STEPS):
        current = jnp.arange(rows_all, dtype=jnp.int32)
        lineage_list = [current]
        for earlier in range(later_step, 0, -1):
            current = source_start + parents[earlier][current]
            lineage_list.append(current)
        lineage_list = lineage_list[::-1] + [current] * (STEPS - later_step - 1)
        lineage.append(jnp.stack(lineage_list))
        root_table.append(source_start + parents[0][current])
    return (jnp.stack(lineage), jnp.stack(root_table))


def per_device(
    step_inputs,
    norm_gain,
    query_weight,
    kv_weight,
    out_weight,
    kv_cache,
    block_table,
    prefix_len,
    parents,
):
    segments = lax.axis_size("segment")
    segment_id = lax.axis_index("segment")
    device_id = lax.axis_index("tensor")
    local_width = step_inputs.shape[2]
    rows_all = step_inputs.shape[1]
    head_count = query_weight.shape[2] // HEAD_SIZE
    kv_owner = device_id * head_count // GROUP
    score_scale = HEAD_SIZE ** (-0.5)
    lineage, root_table = ancestry(parents)
    gain = norm_gain[0]
    query_local = query_weight[0]
    kv_local = kv_weight[0]
    out_local = out_weight[0]
    cache_local = kv_cache[0, 0]

    def project_rows(piece):
        return jnp.dot(piece, out_local, preferred_element_type=jnp.float32)

    def advance(loop_state, tick_index, item_base, item_count):
        incoming, history, received = loop_state
        local_item = tick_index - segment_id
        active = (local_item >= 0) & (local_item < item_count)
        item_index = item_base + jnp.clip(local_item, 0, item_count - 1)
        step_index = item_index // SOURCES
        source = item_index % SOURCES
        row_start = source * BEAMS
        fresh_rows = lax.dynamic_slice(
            step_inputs, (step_index, row_start, 0), (1, BEAMS, local_width)
        )[0]
        current = jnp.where(segment_id == 0, fresh_rows, incoming)
        full_rows = lax.all_gather(current, "tensor", axis=1, tiled=True)
        normed = normalize(full_rows, gain)
        queries = jnp.dot(normed, query_local, preferred_element_type=jnp.float32).reshape(
            BEAMS, head_count, HEAD_SIZE
        )
        partial_kv = jnp.einsum(
            "rd,dkc->rkc", normed, kv_local, preferred_element_type=jnp.float32
        ).astype(jnp.bfloat16)
        gathered_kv = lax.all_gather(partial_kv, "tensor", axis=2, tiled=True)
        gathered_kv = gathered_kv.reshape(BEAMS, 2, HEAD_SIZE, KV_HEADS)
        own_kv = lax.dynamic_slice_in_dim(gathered_kv, kv_owner, 1, 3)[..., 0]
        lineage_rows = lax.dynamic_slice(lineage, (step_index, 0, row_start), (1, STEPS, BEAMS))[0]
        root_rows = lax.dynamic_slice(root_table, (step_index, row_start), (1, BEAMS))[0]
        lengths = prefix_len[root_rows]
        positions = lengths + step_index
        new_key = rotate(own_kv[:, 0:1].astype(jnp.float32), positions).astype(jnp.bfloat16)[:, 0]
        turned_query = rotate(queries, positions).astype(jnp.bfloat16)
        new_entry = jnp.stack([new_key, own_kv[:, 1]], axis=1)
        updated = lax.dynamic_update_slice(history, new_entry[None], (step_index, row_start, 0, 0))
        history = jnp.where(active, updated, history)
        past = history[jnp.arange(STEPS, dtype=jnp.int32)[:, None], lineage_rows]
        history_mask = jnp.arange(STEPS, dtype=jnp.int32) <= step_index
        prefix_mask = jnp.arange(2 * BLOCK, dtype=jnp.int32)[None, :] < lengths[:, None]
        table_rows = block_table[root_rows]
        blocks = cache_local[table_rows].reshape(BEAMS, 2 * BLOCK, 2 * HEAD_SIZE)
        prefix_scores = jnp.einsum(
            "rhd,rkd->rhk",
            turned_query,
            blocks[:, :, :HEAD_SIZE],
            preferred_element_type=jnp.float32,
        )
        prefix_scores = jnp.where(prefix_mask[:, None, :], prefix_scores * score_scale, MASK_FLOOR)
        history_scores = (
            jnp.einsum(
                "rhd,trd->rht", turned_query, past[:, :, 0], preferred_element_type=jnp.float32
            )
            * score_scale
        )
        history_scores = jnp.where(history_mask[None, None, :], history_scores, MASK_FLOOR)
        highest = jnp.maximum(jnp.max(prefix_scores, axis=-1), jnp.max(history_scores, axis=-1))[
            ..., None
        ]
        prefix_exp = jnp.exp(prefix_scores - highest)
        history_exp = jnp.exp(history_scores - highest)
        denominator = jnp.sum(prefix_exp, axis=-1, keepdims=True) + jnp.sum(
            history_exp, axis=-1, keepdims=True
        )
        prefix_probs = (prefix_exp / denominator).astype(jnp.bfloat16)
        history_probs = (history_exp / denominator).astype(jnp.bfloat16)
        mixture = jnp.einsum(
            "rhk,rkd->rhd",
            prefix_probs,
            blocks[:, :, HEAD_SIZE:],
            preferred_element_type=jnp.float32,
        )
        mixture = mixture + jnp.einsum(
            "rht,trd->rhd", history_probs, past[:, :, 1], preferred_element_type=jnp.float32
        )
        attended = mixture.reshape(BEAMS, head_count * HEAD_SIZE).astype(jnp.bfloat16)
        update = project_rows(lax.all_gather(attended, "tensor", axis=1, tiled=True))
        result = (current.astype(jnp.float32) + update).astype(jnp.bfloat16)
        passed = shifted(result, "segment", 1)
        sender = (segment_id + segments - 1) % segments
        sent_local = tick_index - sender
        sent_valid = (sent_local >= 0) & (sent_local < item_count)
        sent_item = item_base + jnp.clip(sent_local, 0, item_count - 1)
        sent_step = sent_item // SOURCES
        sent_row = sent_item % SOURCES * BEAMS
        stored = lax.dynamic_update_slice(received, passed[None], (sent_step, sent_row, 0))
        received = jnp.where(sent_valid, stored, received)
        return (passed, history, received)

    loop_state = (
        jnp.zeros((BEAMS, local_width), jnp.bfloat16),
        jnp.zeros((STEPS, rows_all, 2, HEAD_SIZE), jnp.bfloat16),
        jnp.zeros((STEPS, rows_all, local_width), jnp.bfloat16),
    )
    sweep_loop_state = loop_state
    item_count = STEPS * SOURCES

    def scan_step(state_in, tick_index):
        return (advance(state_in, tick_index, 0, item_count), None)

    ticks = jnp.arange(item_count + segments - 1, dtype=jnp.int32)
    sweep_loop_state, unused = lax.scan(scan_step, sweep_loop_state, ticks)
    loop_state = sweep_loop_state
    return loop_state[2][None]


def solution(mesh):
    return jax.shard_map(
        per_device,
        mesh=mesh,
        in_specs=(
            P(None, None, "tensor"),
            P("segment", None),
            P("segment", None, "tensor"),
            P("segment", None, None, "tensor"),
            P("segment", None, "tensor"),
            P("segment", "tensor", None, None, None),
            P(),
            P(),
            P(),
        ),
        out_specs=P("segment", None, None, "tensor"),
        check_vma=False,
    )
```

profile of v0, /device:TPU:0, one launch (start us, length us, event | category | flops | bytes accessed | tf_op | source)
XLA Modules:
  0.0 343.2 jit_solution(172588675042118891)
XLA Ops:
  0.1 0.9 slice_bitcast_fusion
  0.9 0.7 gather_fusion.7
  1.6 0.7 gather_fusion.8
  2.3 0.7 gather_fusion.9
  3.0 0.7 gather_fusion.5
  3.7 0.7 gather_fusion.6
  4.4 0.7 gather_fusion.4
  5.4 337.2 %while.17 = (s32[]{:T(128)}, bf16[16,512]{1,0:T(8,128)(2,1)S(1)}, bf16[3,16,2,128]{3,2,1,0:T(2,128)(2,1)S(1)}, bf16[3,16,512]{2,1,0:T(8,128)(2,1)S(1)}, pred[]{:...) while((s32[]{:T(128)}, bf16[16,512]{1,0:T(8,128)(2,1)S(1)}, ...), condition=%wide.region_6.7_spmd, body=%wide.region_0.6_spmd.sunk | while | flops 312203328 | bytes 28216092 | solution.py:184
  6.7 0.7 gather_fusion.2
  7.4 0.7 bitcast_select_fusion.3
  8.1 23.8 %all_gather.24 = bf16[16,8192]{1,0:T(8,128)(2,1)S(1)} all-gather(bf16[16,512]{1,0:T(8,128)(2,1)S(1)} %bitcast_select_fusion.3), channel_id=1, replica_groups=mesh['segment'=2,'tensor'=16] {'tensor'}, dimensions={1}, use_global_device_ids=true | all-gather | bytes 278528 | tf_op jit(solution)/shard_map/while/body/eval_jaxpr/all_gather | solution.py:100
  32.1 0.9 convolution_convert_fusion.2
  33.2 18.9 %all_gather.25 = bf16[16,2,1024]{0,1,2:T(2,128)(2,1)S(1)} all-gather(bf16[16,2,64]{0,1,2:T(2,128)(2,1)S(1)} %copy.77), channel_id=1, replica_groups=mesh['segment'=2,'tensor'=16] {'tensor'}, dimensions={2}, use_global_device_ids=true | all-gather | bytes 69632 | tf_op jit(solution)/shard_map/while/body/eval_jaxpr/all_gather | solution.py:108
  53.2 0.9 gather_fusion.3
  54.1 4.6 %fusion.83 = f32[16,512]{1,0:T(8,128)S(1)} fusion(bf16[8192,512]{1,0:T(8,128)(2,1)} %get-tuple-element.631, bf16[16,8192]{1,0:T(8,128)(2,1)S(1)} %all_gather.24, f32[8192]{0:T(1024)S(1)} %bitcast.161, f32[16]{0:T(128)S(1)} %add_rsqrt_fusion.2), kind=kOutput, calls=%fused_computation.31.clone.1 | convolution fusion | flops 134742016 | bytes 8716352 | tf_op jit(solution)/shard_map/while/body/eval_jaxpr/dot_general | solution.py:102
  59.7 2.0 gather_fusion.1
  62.0 1.7 fusion.86
  63.9 1.5 fusion.94
  65.7 19.5 %all_gather.26 = bf16[16,8192]{1,0:T(8,128)(2,1)S(1)} all-gather(bf16[16,512]{1,0:T(8,128)(2,1)S(1)} %bitcast.164), channel_id=1, replica_groups=mesh['segment'=2,'tensor'=16] {'tensor'}, dimensions={1}, use_global_device_ids=true | all-gather | bytes 278528 | tf_op jit(solution)/shard_map/while/body/eval_jaxpr/all_gather | solution.py:159
  85.2 4.6 %fusion.96 = bf16[16,512]{1,0:T(8,128)(2,1)S(1)} fusion(bf16[16,8192]{1,0:T(8,128)(2,1)S(1)} %all_gather.26, bf16[8192,512]{1,0:T(8,128)(2,1)} %get-tuple-element.637, bf16[16,512]{1,0:T(8,128)(2,1)S(1)} %bitcast_select_fusion.3), kind=kOutput, calls=%fused_computation.17.clone.1 | convolution fusion | flops 134242304 | bytes 8683520 | tf_op jit(solution)/shard_map/while/body/eval_jaxpr/dot_general | solution.py:86
  89.8 1.5 collective-permute-start
  91.9 1.6 collective-permute-done
  94.9 0.7 gather_fusion.2
  95.6 0.7 bitcast_select_fusion.3
  96.3 18.2 %all_gather.24 = bf16[16,8192]{1,0:T(8,128)(2,1)S(1)} all-gather(bf16[16,512]{1,0:T(8,128)(2,1)S(1)} %bitcast_select_fusion.3), channel_id=1, replica_groups=mesh['segment'=2,'tensor'=16] {'tensor'}, dimensions={1}, use_global_device_ids=true | all-gather | bytes 278528 | tf_op jit(solution)/shard_map/while/body/eval_jaxpr/all_gather | solution.py:100
  114.7 0.9 convolution_convert_fusion.2
  115.8 20.3 %all_gather.25 = bf16[16,2,1024]{0,1,2:T(2,128)(2,1)S(1)} all-gather(bf16[16,2,64]{0,1,2:T(2,128)(2,1)S(1)} %copy.77), channel_id=1, replica_groups=mesh['segment'=2,'tensor'=16] {'tensor'}, dimensions={2}, use_global_device_ids=true | all-gather | bytes 69632 | tf_op jit(solution)/shard_map/while/body/eval_jaxpr/all_gather | solution.py:108
  137.2 0.9 gather_fusion.3
  138.1 4.6 %fusion.83 = f32[16,512]{1,0:T(8,128)S(1)} fusion(bf16[8192,512]{1,0:T(8,128)(2,1)} %get-tuple-element.631, bf16[16,8192]{1,0:T(8,128)(2,1)S(1)} %all_gather.24, f32[8192]{0:T(1024)S(1)} %bitcast.161, f32[16]{0:T(128)S(1)} %add_rsqrt_fusion.2), kind=kOutput, calls=%fused_computation.31.clone.1 | convolution fusion | flops 134742016 | bytes 8716352 | tf_op jit(solution)/shard_map/while/body/eval_jaxpr/dot_general | solution.py:102
  143.7 2.0 gather_fusion.1
  146.0 1.7 fusion.86
  147.9 1.5 fusion.94
  149.7 18.2 %all_gather.26 = bf16[16,8192]{1,0:T(8,128)(2,1)S(1)} all-gather(bf16[16,512]{1,0:T(8,128)(2,1)S(1)} %bitcast.164), channel_id=1, replica_groups=mesh['segment'=2,'tensor'=16] {'tensor'}, dimensions={1}, use_global_device_ids=true | all-gather | bytes 278528 | tf_op jit(solution)/shard_map/while/body/eval_jaxpr/all_gather | solution.py:159
  167.8 4.6 %fusion.96 = bf16[16,512]{1,0:T(8,128)(2,1)S(1)} fusion(bf16[16,8192]{1,0:T(8,128)(2,1)S(1)} %all_gather.26, bf16[8192,512]{1,0:T(8,128)(2,1)} %get-tuple-element.637, bf16[16,512]{1,0:T(8,128)(2,1)S(1)} %bitcast_select_fusion.3), kind=kOutput, calls=%fused_computation.17.clone.1 | convolution fusion | flops 134242304 | bytes 8683520 | tf_op jit(solution)/shard_map/while/body/eval_jaxpr/dot_general | solution.py:86
  172.4 1.5 collective-permute-start
  174.5 1.6 collective-permute-done
  177.4 0.7 gather_fusion.2
  178.2 0.7 bitcast_select_fusion.3
  178.9 19.5 %all_gather.24 = bf16[16,8192]{1,0:T(8,128)(2,1)S(1)} all-gather(bf16[16,512]{1,0:T(8,128)(2,1)S(1)} %bitcast_select_fusion.3), channel_id=1, replica_groups=mesh['segment'=2,'tensor'=16] {'tensor'}, dimensions={1}, use_global_device_ids=true | all-gather | bytes 278528 | tf_op jit(solution)/shard_map/while/body/eval_jaxpr/all_gather | solution.py:100
  198.6 0.9 convolution_convert_fusion.2
  199.6 18.9 %all_gather.25 = bf16[16,2,1024]{0,1,2:T(2,128)(2,1)S(1)} all-gather(bf16[16,2,64]{0,1,2:T(2,128)(2,1)S(1)} %copy.77), channel_id=1, replica_groups=mesh['segment'=2,'tensor'=16] {'tensor'}, dimensions={2}, use_global_device_ids=true | all-gather | bytes 69632 | tf_op jit(solution)/shard_map/while/body/eval_jaxpr/all_gather | solution.py:108
  219.7 0.9 gather_fusion.3
  220.6 4.6 %fusion.83 = f32[16,512]{1,0:T(8,128)S(1)} fusion(bf16[8192,512]{1,0:T(8,128)(2,1)} %get-tuple-element.631, bf16[16,8192]{1,0:T(8,128)(2,1)S(1)} %all_gather.24, f32[8192]{0:T(1024)S(1)} %bitcast.161, f32[16]{0:T(128)S(1)} %add_rsqrt_fusion.2), kind=kOutput, calls=%fused_computation.31.clone.1 | convolution fusion | flops 134742016 | bytes 8716352 | tf_op jit(solution)/shard_map/while/body/eval_jaxpr/dot_general | solution.py:102
  226.2 2.0 gather_fusion.1
  228.4 1.7 fusion.86
  230.4 1.5 fusion.94
  232.1 19.5 %all_gather.26 = bf16[16,8192]{1,0:T(8,128)(2,1)S(1)} all-gather(bf16[16,512]{1,0:T(8,128)(2,1)S(1)} %bitcast.164), channel_id=1, replica_groups=mesh['segment'=2,'tensor'=16] {'tensor'}, dimensions={1}, use_global_device_ids=true | all-gather | bytes 278528 | tf_op jit(solution)/shard_map/while/body/eval_jaxpr/all_gather | solution.py:159
  251.6 4.6 %fusion.96 = bf16[16,512]{1,0:T(8,128)(2,1)S(1)} fusion(bf16[16,8192]{1,0:T(8,128)(2,1)S(1)} %all_gather.26, bf16[8192,512]{1,0:T(8,128)(2,1)} %get-tuple-element.637, bf16[16,512]{1,0:T(8,128)(2,1)S(1)} %bitcast_select_fusion.3), kind=kOutput, calls=%fused_computation.17.clone.1 | convolution fusion | flops 134242304 | bytes 8683520 | tf_op jit(solution)/shard_map/while/body/eval_jaxpr/dot_general | solution.py:86
  256.2 1.5 collective-permute-start
  258.3 1.6 collective-permute-done
  261.2 0.7 gather_fusion.2
  262.0 0.7 bitcast_select_fusion.3
  262.7 18.2 %all_gather.24 = bf16[16,8192]{1,0:T(8,128)(2,1)S(1)} all-gather(bf16[16,512]{1,0:T(8,128)(2,1)S(1)} %bitcast_select_fusion.3), channel_id=1, replica_groups=mesh['segment'=2,'tensor'=16] {'tensor'}, dimensions={1}, use_global_device_ids=true | all-gather | bytes 278528 | tf_op jit(solution)/shard_map/while/body/eval_jaxpr/all_gather | solution.py:100
  281.1 0.9 convolution_convert_fusion.2
  282.2 20.3 %all_gather.25 = bf16[16,2,1024]{0,1,2:T(2,128)(2,1)S(1)} all-gather(bf16[16,2,64]{0,1,2:T(2,128)(2,1)S(1)} %copy.77), channel_id=1, replica_groups=mesh['segment'=2,'tensor'=16] {'tensor'}, dimensions={2}, use_global_device_ids=true | all-gather | bytes 69632 | tf_op jit(solution)/shard_map/while/body/eval_jaxpr/all_gather | solution.py:108
  303.6 0.9 gather_fusion.3
  304.5 4.6 %fusion.83 = f32[16,512]{1,0:T(8,128)S(1)} fusion(bf16[8192,512]{1,0:T(8,128)(2,1)} %get-tuple-element.631, bf16[16,8192]{1,0:T(8,128)(2,1)S(1)} %all_gather.24, f32[8192]{0:T(1024)S(1)} %bitcast.161, f32[16]{0:T(128)S(1)} %add_rsqrt_fusion.2), kind=kOutput, calls=%fused_computation.31.clone.1 | convolution fusion | flops 134742016 | bytes 8716352 | tf_op jit(solution)/shard_map/while/body/eval_jaxpr/dot_general | solution.py:102
  310.1 2.0 gather_fusion.1
  312.3 1.7 fusion.86
  314.3 1.5 fusion.94
  316.0 18.2 %all_gather.26 = bf16[16,8192]{1,0:T(8,128)(2,1)S(1)} all-gather(bf16[16,512]{1,0:T(8,128)(2,1)S(1)} %bitcast.164), channel_id=1, replica_groups=mesh['segment'=2,'tensor'=16] {'tensor'}, dimensions={1}, use_global_device_ids=true | all-gather | bytes 278528 | tf_op jit(solution)/shard_map/while/body/eval_jaxpr/all_gather | solution.py:159
  334.2 4.6 %fusion.96 = bf16[16,512]{1,0:T(8,128)(2,1)S(1)} fusion(bf16[16,8192]{1,0:T(8,128)(2,1)S(1)} %all_gather.26, bf16[8192,512]{1,0:T(8,128)(2,1)} %get-tuple-element.637, bf16[16,512]{1,0:T(8,128)(2,1)S(1)} %bitcast_select_fusion.3), kind=kOutput, calls=%fused_computation.17.clone.1 | convolution fusion | flops 134242304 | bytes 8683520 | tf_op jit(solution)/shard_map/while/body/eval_jaxpr/dot_general | solution.py:86
  338.8 1.5 collective-permute-start
  340.9 1.6 collective-permute-done
  (205 shorter events, 16.0 us)
Async XLA Ops:
  0.0 5.2 %copy-start.5 = (s32[16,2]{0,1:T(2,128)S(1)}, s32[16,2]{0,1:T(2,128)}, u32[]{:S(2)}) copy-start(s32[16,2]{0,1:T(2,128)} %param.17) | copy-start | bytes 388
  0.0 5.3 %copy-start.1 = (bf16[1,1,3,128,256]{4,3,2,1,0:T(8,128)(2,1)S(1)}, bf16[1,1,3,128,256]{4,3,2,1,0:T(8,128)(2,1)}, u32[]{:S(2)}) copy-start(bf16[1,1,3,128,256]{4,3,2,1,0:T(8,128)(2,1)} %param.16) | copy-start | bytes 589828
  0.0 5.3 %copy-start.2 = (bf16[1,8192,2,64]{1,3,2,0:T(8,128)(2,1)S(1)}, bf16[1,8192,2,64]{1,3,2,0:T(8,128)(2,1)}, u32[]{:S(2)}) copy-start(bf16[1,8192,2,64]{1,3,2,0:T(8,128)(2,1)} %param.14) | copy-start | bytes 6291460
  0.0 5.3 %copy-start.3 = (f32[1,8192]{1,0:T(1,128)S(1)}, f32[1,8192]{1,0:T(1,128)}, u32[]{:S(2)}) copy-start(f32[1,8192]{1,0:T(1,128)} %param.12) | copy-start | bytes 98308
  0.0 5.3 %copy-start = (s32[16]{0:T(128)S(1)}, s32[16]{0:T(128)}, u32[]{:S(2)}) copy-start(s32[16]{0:T(128)} %param.18) | copy-start | bytes 196
  89.8 3.8 %collective-permute-start = (bf16[16,512]{1,0:T(8,128)(2,1)S(1)}, bf16[16,512]{1,0:T(8,128)(2,1)S(1)}, u32[]{:S(2)}, u32[]{:S(2)}) collective-permute-start(bf16[16,512]{1,0:T(8,128)(2,1)S(1)} %fusion.96), channel_id=1, source_target_pairs={{16,0},{0,16},{17,1},{1,17},{18,2},{2,18},{19,3},{3,19},{20,4},{4,... | collective-permute-start | bytes 49160 | tf_op jit(solution)/shard_map/while/body/eval_jaxpr/ppermute | solution.py:21
  172.4 3.8 %collective-permute-start = (bf16[16,512]{1,0:T(8,128)(2,1)S(1)}, bf16[16,512]{1,0:T(8,128)(2,1)S(1)}, u32[]{:S(2)}, u32[]{:S(2)}) collective-permute-start(bf16[16,512]{1,0:T(8,128)(2,1)S(1)} %fusion.96), channel_id=1, source_target_pairs={{16,0},{0,16},{17,1},{1,17},{18,2},{2,18},{19,3},{3,19},{20,4},{4,... | collective-permute-start | bytes 49160 | tf_op jit(solution)/shard_map/while/body/eval_jaxpr/ppermute | solution.py:21
  256.2 3.8 %collective-permute-start = (bf16[16,512]{1,0:T(8,128)(2,1)S(1)}, bf16[16,512]{1,0:T(8,128)(2,1)S(1)}, u32[]{:S(2)}, u32[]{:S(2)}) collective-permute-start(bf16[16,512]{1,0:T(8,128)(2,1)S(1)} %fusion.96), channel_id=1, source_target_pairs={{16,0},{0,16},{17,1},{1,17},{18,2},{2,18},{19,3},{3,19},{20,4},{4,... | collective-permute-start | bytes 49160 | tf_op jit(solution)/shard_map/while/body/eval_jaxpr/ppermute | solution.py:21
  338.8 3.8 %collective-permute-start = (bf16[16,512]{1,0:T(8,128)(2,1)S(1)}, bf16[16,512]{1,0:T(8,128)(2,1)S(1)}, u32[]{:S(2)}, u32[]{:S(2)}) collective-permute-start(bf16[16,512]{1,0:T(8,128)(2,1)S(1)} %fusion.96), channel_id=1, source_target_pairs={{16,0},{0,16},{17,1},{1,17},{18,2},{2,18},{19,3},{3,19},{20,4},{4,... | collective-permute-start | bytes 49160 | tf_op jit(solution)/shard_map/while/body/eval_jaxpr/ppermute | solution.py:21
  342.5 0.6 copy-start.4
where the time goes:
time: 344 us; the launch traced here: 343 us
  blocking collectives  233 us (68%)
  matrix products  54.9 us (16%)
  local copies, waits for them, and re-layouts  27.8 us (8%)
  other arithmetic  8.74 us (3%)
  waiting for transfers between devices  6.44 us (2%)
  starting transfers between devices  6.02 us (2%)
  loops' own time  5.8 us (2%)
    all_gather x4, blocking collectives, advance(): full_rows = lax.all_gather(current, 'tensor', axis=1, tiled=True)  79.6 us
    all_gather x4, blocking collectives, advance(): gathered_kv = lax.all_gather(partial_kv, 'tensor', axis=2, tiled=True)  78.3 us
    all_gather x4, blocking collectives, advance(): lax.all_gather(attended, 'tensor', axis=1, tiled=True)  75.3 us
    dot_general x4, matrix products, advance(): jnp.dot(normed, query_local, preferred_element_type=jnp.float32)  18.5 us
    dot_general x4, matrix products, project_rows(): return jnp.dot(piece, out_local, preferred_element_type=jnp.float32)  18.3 us
    gather x4, local copies, waits for them, and re-layouts, advance(): blocks = cache_local[table_rows].reshape(BEAMS, 2 * BLOCK, 2 * HEAD_SIZE)  8.11 us
  transfers between devices with their start and end apart: 4, of which 4 were waited for; matrix products, arithmetic and copies ran while one was open for 0% of the time, Pallas kernels for 0%

commit v1 on v0

--- a/solution.py
+++ b/solution.py
@@ -13,6 +13,18 @@
 ROPE_BASE = 1000000.0
 NORM_EPS = 1e-06
 MASK_FLOOR = -1e30
+
+
+def doubled_up(shard, axis, dim):
+    ways, here = (lax.axis_size(axis), lax.axis_index(axis))
+    grown, reach = (shard, 1)
+    while reach < ways:
+        theirs = lax.ppermute(grown, axis, [(d, d ^ reach) for d in range(ways)])
+        mine_first = jnp.concatenate([grown, theirs], axis=dim)
+        theirs_first = jnp.concatenate([theirs, grown], axis=dim)
+        grown = jnp.where(here & reach == 0, mine_first, theirs_first)
+        reach = 2 * reach
+    return grown
 
 
 def shifted(block, axis, distance):
@@ -105,7 +117,7 @@
         partial_kv = jnp.einsum(
             "rd,dkc->rkc", normed, kv_local, preferred_element_type=jnp.float32
         ).astype(jnp.bfloat16)
-        gathered_kv = lax.all_gather(partial_kv, "tensor", axis=2, tiled=True)
+        gathered_kv = doubled_up(partial_kv, "tensor", 2)
         gathered_kv = gathered_kv.reshape(BEAMS, 2, HEAD_SIZE, KV_HEADS)
         own_kv = lax.dynamic_slice_in_dim(gathered_kv, kv_owner, 1, 3)[..., 0]
         lineage_rows = lax.dynamic_slice(lineage, (step_index, 0, row_start), (1, STEPS, BEAMS))[0]

time: 344 us -> 318 us (0.924)
  blocking collectives: 233 us -> 155 us
  waiting for transfers between devices: 6.44 us -> 53.1 us
    all_gather x4 -> x0, blocking collectives: 78.3 us -> none  [advance(): gathered_kv = lax.all_gather(partial_kv, 'tensor', axis=2, tiled=True)]
    ppermute x0 -> x16, waiting for transfers between devices: none -> 46.7 us  [doubled_up(): theirs = lax.ppermute(grown, axis, [(d, d ^ reach) for d in range(ways)])]
    all_gather x4, blocking collectives: 75.3 us -> 71.4 us  [advance(): lax.all_gather(attended, 'tensor', axis=1, tiled=True)]
    all_gather x4, blocking collectives: 79.6 us -> 83.5 us  [advance(): full_rows = lax.all_gather(current, 'tensor', axis=1, tiled=True)]
  transfers between devices with their start and end apart: 4 -> 20, of which waited for: 4 -> 16; matrix products, arithmetic and copies ran while one was open for 0% -> 14% of each run, Pallas kernels for 0% -> 0%
where the time goes in v1:
time: 318 us; the launch traced here: 317 us
  blocking collectives  155 us (49%)
  matrix products  54.9 us (17%)
  waiting for transfers between devices  53.1 us (17%)
  local copies, waits for them, and re-layouts  29.1 us (9%)
  other arithmetic  10.9 us (3%)
  starting transfers between devices  7.83 us (2%)
  loops' own time  6.08 us (2%)
    all_gather x4, blocking collectives, advance(): full_rows = lax.all_gather(current, 'tensor', axis=1, tiled=True)  83.5 us
    all_gather x4, blocking collectives, advance(): lax.all_gather(attended, 'tensor', axis=1, tiled=True)  71.4 us
    ppermute x16, waiting for transfers between devices, doubled_up(): theirs = lax.ppermute(grown, axis, [(d, d ^ reach) for d in range(ways)])  46.7 us
    dot_general x4, matrix products, advance(): jnp.dot(normed, query_local, preferred_element_type=jnp.float32)  18.5 us
    dot_general x4, matrix products, project_rows(): return jnp.dot(piece, out_local, preferred_element_type=jnp.float32)  18.3 us
    gather x4, local copies, waits for them, and re-layouts, advance(): blocks = cache_local[table_rows].reshape(BEAMS, 2 * BLOCK, 2 * HEAD_SIZE)  8.03 us
    dot_general x4, matrix products, advance(): jnp.einsum('rhd,rkd->rhk', turned_query, blocks[:, :, :HEAD_SIZE], prefer...  6.74 us
    ppermute x4, waiting for transfers between devices, shifted(): return lax.ppermute(block, axis, route)  6.4 us
  transfers between devices with their start and end apart: 20, of which 16 were waited for; matrix products, arithmetic and copies ran while one was open for 14% of the time, Pallas kernels for 0%

profile of v1, /device:TPU:0, one launch (start us, length us, event | category | flops | bytes accessed | tf_op | source)
XLA Modules:
  0.0 317.1 jit_solution(5508007048366915790)
XLA Ops:
  0.1 0.9 slice_bitcast_fusion
  3.0 0.7 gather_fusion.5
  4.4 0.7 gather_fusion.4
  5.4 311.1 %while.17 = (s32[]{:T(128)}, bf16[16,512]{1,0:T(8,128)(2,1)S(1)}, bf16[3,16,2,128]{3,2,1,0:T(2,128)(2,1)S(1)}, bf16[3,16,512]{2,1,0:T(8,128)(2,1)S(1)}, pred[]{:...) while((s32[]{:T(128)}, bf16[16,512]{1,0:T(8,128)(2,1)S(1)}, ...), condition=%wide.region_6.7_spmd, body=%wide.region_0.6_spmd.sunk | while | flops 312584256 | bytes 28671032 | solution.py:196
  6.7 0.7 bitcast_select_fusion.3
  7.4 23.8 %all_gather.16 = bf16[16,8192]{1,0:T(8,128)(2,1)S(1)} all-gather(bf16[16,512]{1,0:T(8,128)(2,1)S(1)} %bitcast_select_fusion.3), channel_id=1, replica_groups=mesh['segment'=2,'tensor'=16] {'tensor'}, dimensions={1}, use_global_device_ids=true | all-gather | bytes 278528 | tf_op jit(solution)/shard_map/while/body/eval_jaxpr/all_gather | solution.py:112
  31.4 0.9 convolution_convert_fusion.2
  33.5 4.6 %fusion.85 = f32[16,512]{1,0:T(8,128)S(1)} fusion(bf16[8192,512]{1,0:T(8,128)(2,1)} %get-tuple-element.675, bf16[16,8192]{1,0:T(8,128)(2,1)S(1)} %all_gather.16, f32[8192]{0:T(1024)S(1)} %bitcast.173, f32[16]{0:T(128)S(1)} %add_rsqrt_fusion.2), kind=kOutput, calls=%fused_computation.40.clone.1 | convolution fusion | flops 134742016 | bytes 8716352 | tf_op jit(solution)/shard_map/while/body/eval_jaxpr/dot_general | solution.py:114
  39.3 2.0 gather_fusion.1
  41.4 1.7 fusion.88
  43.5 3.5 %collective-permute-done.1 = bf16[16,2,128]{2,0,1:T(8,128)(2,1)S(1)} collective-permute-done((bf16[16,2,128]{2,0,1:T(8,128)(2,1)S(1)}, bf16[16,2,128]{2,0,1:T(8,128)(2,1)S(1)}, u32[]{:S(2)}, u32[]{:S(2)}) %collective-permute-start.1) | collective-permute-done | bytes 8224 | tf_op jit(solution)/shard_map/while/body/eval_jaxpr/ppermute | solution.py:22
  47.2 3.6 %collective-permute-done.2 = bf16[16,2,256]{2,0,1:T(8,128)(2,1)S(1)} collective-permute-done((bf16[16,2,256]{2,0,1:T(8,128)(2,1)S(1)}, bf16[16,2,256]{2,0,1:T(8,128)(2,1)S(1)}, u32[]{:S(2)}, u32[]{:S(2)}) %collective-permute-start.2) | collective-permute-done | bytes 16416 | tf_op jit(solution)/shard_map/while/body/eval_jaxpr/ppermute | solution.py:22
  51.1 4.6 %collective-permute-done.3 = bf16[16,2,512]{2,0,1:T(8,128)(2,1)S(1)} collective-permute-done((bf16[16,2,512]{2,0,1:T(8,128)(2,1)S(1)}, bf16[16,2,512]{2,0,1:T(8,128)(2,1)S(1)}, u32[]{:S(2)}, u32[]{:S(2)}) %collective-permute-start.3) | collective-permute-done | bytes 32800 | tf_op jit(solution)/shard_map/while/body/eval_jaxpr/ppermute | solution.py:22
  56.8 0.9 gather_fusion.3
  58.1 1.5 fusion.96
  59.9 17.8 %all_gather.17 = bf16[16,8192]{1,0:T(8,128)(2,1)S(1)} all-gather(bf16[16,512]{1,0:T(8,128)(2,1)S(1)} %bitcast.178), channel_id=1, replica_groups=mesh['segment'=2,'tensor'=16] {'tensor'}, dimensions={1}, use_global_device_ids=true | all-gather | bytes 278528 | tf_op jit(solution)/shard_map/while/body/eval_jaxpr/all_gather | solution.py:171
  77.7 4.6 %fusion.98 = bf16[16,512]{1,0:T(8,128)(2,1)S(1)} fusion(bf16[16,8192]{1,0:T(8,128)(2,1)S(1)} %all_gather.17, bf16[8192,512]{1,0:T(8,128)(2,1)} %get-tuple-element.681, bf16[16,512]{1,0:T(8,128)(2,1)S(1)} %bitcast_select_fusion.3), kind=kOutput, calls=%fused_computation.17.clone.1 | convolution fusion | flops 134242304 | bytes 8683520 | tf_op jit(solution)/shard_map/while/body/eval_jaxpr/dot_general | solution.py:98
  82.3 1.5 collective-permute-start.4
  84.5 1.6 collective-permute-done.4
  87.4 0.7 bitcast_select_fusion.3
  88.1 19.9 %all_gather.16 = bf16[16,8192]{1,0:T(8,128)(2,1)S(1)} all-gather(bf16[16,512]{1,0:T(8,128)(2,1)S(1)} %bitcast_select_fusion.3), channel_id=1, replica_groups=mesh['segment'=2,'tensor'=16] {'tensor'}, dimensions={1}, use_global_device_ids=true | all-gather | bytes 278528 | tf_op jit(solution)/shard_map/while/body/eval_jaxpr/all_gather | solution.py:112
  108.2 0.9 convolution_convert_fusion.2
  110.3 4.6 %fusion.85 = f32[16,512]{1,0:T(8,128)S(1)} fusion(bf16[8192,512]{1,0:T(8,128)(2,1)} %get-tuple-element.675, bf16[16,8192]{1,0:T(8,128)(2,1)S(1)} %all_gather.16, f32[8192]{0:T(1024)S(1)} %bitcast.173, f32[16]{0:T(128)S(1)} %add_rsqrt_fusion.2), kind=kOutput, calls=%fused_computation.40.clone.1 | convolution fusion | flops 134742016 | bytes 8716352 | tf_op jit(solution)/shard_map/while/body/eval_jaxpr/dot_general | solution.py:114
  116.1 2.0 gather_fusion.1
  118.2 1.7 fusion.88
  120.3 3.5 %collective-permute-done.1 = bf16[16,2,128]{2,0,1:T(8,128)(2,1)S(1)} collective-permute-done((bf16[16,2,128]{2,0,1:T(8,128)(2,1)S(1)}, bf16[16,2,128]{2,0,1:T(8,128)(2,1)S(1)}, u32[]{:S(2)}, u32[]{:S(2)}) %collective-permute-start.1) | collective-permute-done | bytes 8224 | tf_op jit(solution)/shard_map/while/body/eval_jaxpr/ppermute | solution.py:22
  124.0 3.6 %collective-permute-done.2 = bf16[16,2,256]{2,0,1:T(8,128)(2,1)S(1)} collective-permute-done((bf16[16,2,256]{2,0,1:T(8,128)(2,1)S(1)}, bf16[16,2,256]{2,0,1:T(8,128)(2,1)S(1)}, u32[]{:S(2)}, u32[]{:S(2)}) %collective-permute-start.2) | collective-permute-done | bytes 16416 | tf_op jit(solution)/shard_map/while/body/eval_jaxpr/ppermute | solution.py:22
  127.9 4.6 %collective-permute-done.3 = bf16[16,2,512]{2,0,1:T(8,128)(2,1)S(1)} collective-permute-done((bf16[16,2,512]{2,0,1:T(8,128)(2,1)S(1)}, bf16[16,2,512]{2,0,1:T(8,128)(2,1)S(1)}, u32[]{:S(2)}, u32[]{:S(2)}) %collective-permute-start.3) | collective-permute-done | bytes 32800 | tf_op jit(solution)/shard_map/while/body/eval_jaxpr/ppermute | solution.py:22
  133.6 0.9 gather_fusion.3
  134.9 1.5 fusion.96
  136.7 17.8 %all_gather.17 = bf16[16,8192]{1,0:T(8,128)(2,1)S(1)} all-gather(bf16[16,512]{1,0:T(8,128)(2,1)S(1)} %bitcast.178), channel_id=1, replica_groups=mesh['segment'=2,'tensor'=16] {'tensor'}, dimensions={1}, use_global_device_ids=true | all-gather | bytes 278528 | tf_op jit(solution)/shard_map/while/body/eval_jaxpr/all_gather | solution.py:171
  154.5 4.6 %fusion.98 = bf16[16,512]{1,0:T(8,128)(2,1)S(1)} fusion(bf16[16,8192]{1,0:T(8,128)(2,1)S(1)} %all_gather.17, bf16[8192,512]{1,0:T(8,128)(2,1)} %get-tuple-element.681, bf16[16,512]{1,0:T(8,128)(2,1)S(1)} %bitcast_select_fusion.3), kind=kOutput, calls=%fused_computation.17.clone.1 | convolution fusion | flops 134242304 | bytes 8683520 | tf_op jit(solution)/shard_map/while/body/eval_jaxpr/dot_general | solution.py:98
  159.1 1.5 collective-permute-start.4
  161.3 1.6 collective-permute-done.4
  164.2 0.7 bitcast_select_fusion.3
  164.9 19.9 %all_gather.16 = bf16[16,8192]{1,0:T(8,128)(2,1)S(1)} all-gather(bf16[16,512]{1,0:T(8,128)(2,1)S(1)} %bitcast_select_fusion.3), channel_id=1, replica_groups=mesh['segment'=2,'tensor'=16] {'tensor'}, dimensions={1}, use_global_device_ids=true | all-gather | bytes 278528 | tf_op jit(solution)/shard_map/while/body/eval_jaxpr/all_gather | solution.py:112
  185.0 0.9 convolution_convert_fusion.2
  187.1 4.6 %fusion.85 = f32[16,512]{1,0:T(8,128)S(1)} fusion(bf16[8192,512]{1,0:T(8,128)(2,1)} %get-tuple-element.675, bf16[16,8192]{1,0:T(8,128)(2,1)S(1)} %all_gather.16, f32[8192]{0:T(1024)S(1)} %bitcast.173, f32[16]{0:T(128)S(1)} %add_rsqrt_fusion.2), kind=kOutput, calls=%fused_computation.40.clone.1 | convolution fusion | flops 134742016 | bytes 8716352 | tf_op jit(solution)/shard_map/while/body/eval_jaxpr/dot_general | solution.py:114
  192.9 2.0 gather_fusion.1
  195.0 1.7 fusion.88
  197.1 3.5 %collective-permute-done.1 = bf16[16,2,128]{2,0,1:T(8,128)(2,1)S(1)} collective-permute-done((bf16[16,2,128]{2,0,1:T(8,128)(2,1)S(1)}, bf16[16,2,128]{2,0,1:T(8,128)(2,1)S(1)}, u32[]{:S(2)}, u32[]{:S(2)}) %collective-permute-start.1) | collective-permute-done | bytes 8224 | tf_op jit(solution)/shard_map/while/body/eval_jaxpr/ppermute | solution.py:22
  200.8 3.6 %collective-permute-done.2 = bf16[16,2,256]{2,0,1:T(8,128)(2,1)S(1)} collective-permute-done((bf16[16,2,256]{2,0,1:T(8,128)(2,1)S(1)}, bf16[16,2,256]{2,0,1:T(8,128)(2,1)S(1)}, u32[]{:S(2)}, u32[]{:S(2)}) %collective-permute-start.2) | collective-permute-done | bytes 16416 | tf_op jit(solution)/shard_map/while/body/eval_jaxpr/ppermute | solution.py:22
  204.7 4.6 %collective-permute-done.3 = bf16[16,2,512]{2,0,1:T(8,128)(2,1)S(1)} collective-permute-done((bf16[16,2,512]{2,0,1:T(8,128)(2,1)S(1)}, bf16[16,2,512]{2,0,1:T(8,128)(2,1)S(1)}, u32[]{:S(2)}, u32[]{:S(2)}) %collective-permute-start.3) | collective-permute-done | bytes 32800 | tf_op jit(solution)/shard_map/while/body/eval_jaxpr/ppermute | solution.py:22
  210.4 0.9 gather_fusion.3
  211.7 1.5 fusion.96
  213.5 17.8 %all_gather.17 = bf16[16,8192]{1,0:T(8,128)(2,1)S(1)} all-gather(bf16[16,512]{1,0:T(8,128)(2,1)S(1)} %bitcast.178), channel_id=1, replica_groups=mesh['segment'=2,'tensor'=16] {'tensor'}, dimensions={1}, use_global_device_ids=true | all-gather | bytes 278528 | tf_op jit(solution)/shard_map/while/body/eval_jaxpr/all_gather | solution.py:171
  231.3 4.6 %fusion.98 = bf16[16,512]{1,0:T(8,128)(2,1)S(1)} fusion(bf16[16,8192]{1,0:T(8,128)(2,1)S(1)} %all_gather.17, bf16[8192,512]{1,0:T(8,128)(2,1)} %get-tuple-element.681, bf16[16,512]{1,0:T(8,128)(2,1)S(1)} %bitcast_select_fusion.3), kind=kOutput, calls=%fused_computation.17.clone.1 | convolution fusion | flops 134242304 | bytes 8683520 | tf_op jit(solution)/shard_map/while/body/eval_jaxpr/dot_general | solution.py:98
  235.9 1.5 collective-permute-start.4
  238.1 1.6 collective-permute-done.4
  241.0 0.7 bitcast_select_fusion.3
  241.7 19.9 %all_gather.16 = bf16[16,8192]{1,0:T(8,128)(2,1)S(1)} all-gather(bf16[16,512]{1,0:T(8,128)(2,1)S(1)} %bitcast_select_fusion.3), channel_id=1, replica_groups=mesh['segment'=2,'tensor'=16] {'tensor'}, dimensions={1}, use_global_device_ids=true | all-gather | bytes 278528 | tf_op jit(solution)/shard_map/while/body/eval_jaxpr/all_gather | solution.py:112
  261.8 0.9 convolution_convert_fusion.2
  263.9 4.6 %fusion.85 = f32[16,512]{1,0:T(8,128)S(1)} fusion(bf16[8192,512]{1,0:T(8,128)(2,1)} %get-tuple-element.675, bf16[16,8192]{1,0:T(8,128)(2,1)S(1)} %all_gather.16, f32[8192]{0:T(1024)S(1)} %bitcast.173, f32[16]{0:T(128)S(1)} %add_rsqrt_fusion.2), kind=kOutput, calls=%fused_computation.40.clone.1 | convolution fusion | flops 134742016 | bytes 8716352 | tf_op jit(solution)/shard_map/while/body/eval_jaxpr/dot_general | solution.py:114
  269.7 2.0 gather_fusion.1
  271.8 1.7 fusion.88
  273.9 3.5 %collective-permute-done.1 = bf16[16,2,128]{2,0,1:T(8,128)(2,1)S(1)} collective-permute-done((bf16[16,2,128]{2,0,1:T(8,128)(2,1)S(1)}, bf16[16,2,128]{2,0,1:T(8,128)(2,1)S(1)}, u32[]{:S(2)}, u32[]{:S(2)}) %collective-permute-start.1) | collective-permute-done | bytes 8224 | tf_op jit(solution)/shard_map/while/body/eval_jaxpr/ppermute | solution.py:22
  277.6 3.6 %collective-permute-done.2 = bf16[16,2,256]{2,0,1:T(8,128)(2,1)S(1)} collective-permute-done((bf16[16,2,256]{2,0,1:T(8,128)(2,1)S(1)}, bf16[16,2,256]{2,0,1:T(8,128)(2,1)S(1)}, u32[]{:S(2)}, u32[]{:S(2)}) %collective-permute-start.2) | collective-permute-done | bytes 16416 | tf_op jit(solution)/shard_map/while/body/eval_jaxpr/ppermute | solution.py:22
  281.5 4.6 %collective-permute-done.3 = bf16[16,2,512]{2,0,1:T(8,128)(2,1)S(1)} collective-permute-done((bf16[16,2,512]{2,0,1:T(8,128)(2,1)S(1)}, bf16[16,2,512]{2,0,1:T(8,128)(2,1)S(1)}, u32[]{:S(2)}, u32[]{:S(2)}) %collective-permute-start.3) | collective-permute-done | bytes 32800 | tf_op jit(solution)/shard_map/while/body/eval_jaxpr/ppermute | solution.py:22
  287.2 0.9 gather_fusion.3
  288.5 1.5 fusion.96
  290.3 17.8 %all_gather.17 = bf16[16,8192]{1,0:T(8,128)(2,1)S(1)} all-gather(bf16[16,512]{1,0:T(8,128)(2,1)S(1)} %bitcast.178), channel_id=1, replica_groups=mesh['segment'=2,'tensor'=16] {'tensor'}, dimensions={1}, use_global_device_ids=true | all-gather | bytes 278528 | tf_op jit(solution)/shard_map/while/body/eval_jaxpr/all_gather | solution.py:171
  308.1 4.6 %fusion.98 = bf16[16,512]{1,0:T(8,128)(2,1)S(1)} fusion(bf16[16,8192]{1,0:T(8,128)(2,1)S(1)} %all_gather.17, bf16[8192,512]{1,0:T(8,128)(2,1)} %get-tuple-element.681, bf16[16,512]{1,0:T(8,128)(2,1)S(1)} %bitcast_select_fusion.3), kind=kOutput, calls=%fused_computation.17.clone.1 | convolution fusion | flops 134242304 | bytes 8683520 | tf_op jit(solution)/shard_map/while/body/eval_jaxpr/dot_general | solution.py:98
  312.7 1.5 collective-permute-start.4
  314.9 1.6 collective-permute-done.4
  (269 shorter events, 26.7 us)
Async XLA Ops:
  0.0 5.2 %copy-start.5 = (s32[16,2]{0,1:T(2,128)S(1)}, s32[16,2]{0,1:T(2,128)}, u32[]{:S(2)}) copy-start(s32[16,2]{0,1:T(2,128)} %param.17) | copy-start | bytes 388
  0.0 5.3 %copy-start.1 = (bf16[1,1,3,128,256]{4,3,2,1,0:T(8,128)(2,1)S(1)}, bf16[1,1,3,128,256]{4,3,2,1,0:T(8,128)(2,1)}, u32[]{:S(2)}) copy-start(bf16[1,1,3,128,256]{4,3,2,1,0:T(8,128)(2,1)} %param.16) | copy-start | bytes 589828
  0.0 5.3 %copy-start.2 = (bf16[1,8192,2,64]{1,3,2,0:T(8,128)(2,1)S(1)}, bf16[1,8192,2,64]{1,3,2,0:T(8,128)(2,1)}, u32[]{:S(2)}) copy-start(bf16[1,8192,2,64]{1,3,2,0:T(8,128)(2,1)} %param.14) | copy-start | bytes 6291460
  0.0 5.3 %copy-start.3 = (f32[1,8192]{1,0:T(1,128)S(1)}, f32[1,8192]{1,0:T(1,128)}, u32[]{:S(2)}) copy-start(f32[1,8192]{1,0:T(1,128)} %param.12) | copy-start | bytes 98308
  0.0 5.3 %copy-start = (s32[16]{0:T(128)S(1)}, s32[16]{0:T(128)}, u32[]{:S(2)}) copy-start(s32[16]{0:T(128)} %param.18) | copy-start | bytes 196
  32.3 11.0 %collective-permute-start = (bf16[16,2,64]{2,0,1:T(8,128)(2,1)S(1)}, bf16[16,2,64]{2,0,1:T(8,128)(2,1)S(1)}, u32[]{:S(2)}, u32[]{:S(2)}) collective-permute-start(bf16[16,2,64]{2,0,1:T(8,128)(2,1)S(1)} %convolution_convert_fusion.2), channel_id=1, source_target_pairs={{0,1},{1,0},{2,3},{3,2},{4,5},{5,4},{6,7},{7,6},{8,9},{9,8},{10,11... | collective-permute-start | bytes 12296 | tf_op jit(solution)/shard_map/while/body/eval_jaxpr/ppermute | solution.py:22
  43.4 3.7 %collective-permute-start.1 = (bf16[16,2,128]{2,0,1:T(8,128)(2,1)S(1)}, bf16[16,2,128]{2,0,1:T(8,128)(2,1)S(1)}, u32[]{:S(2)}, u32[]{:S(2)}) collective-permute-start(bf16[16,2,128]{2,0,1:T(8,128)(2,1)S(1)} %maximum_select_fusion.12), channel_id=1, source_target_pairs={{0,2},{1,3},{2,0},{3,1},{4,6},{5,7},{6,4},{7,5},{8,10},{9,11},{10,... | collective-permute-start | bytes 24584 | tf_op jit(solution)/shard_map/while/body/eval_jaxpr/ppermute | solution.py:22
  47.1 3.7 %collective-permute-start.2 = (bf16[16,2,256]{2,0,1:T(8,128)(2,1)S(1)}, bf16[16,2,256]{2,0,1:T(8,128)(2,1)S(1)}, u32[]{:S(2)}, u32[]{:S(2)}) collective-permute-start(bf16[16,2,256]{2,0,1:T(8,128)(2,1)S(1)} %maximum_select_fusion.13), channel_id=1, source_target_pairs={{0,4},{1,5},{2,6},{3,7},{4,0},{5,1},{6,2},{7,3},{8,12},{9,13},{10,... | collective-permute-start | bytes 49160 | tf_op jit(solution)/shard_map/while/body/eval_jaxpr/ppermute | solution.py:22
  50.8 4.9 %collective-permute-start.3 = (bf16[16,2,512]{2,0,1:T(8,128)(2,1)S(1)}, bf16[16,2,512]{2,0,1:T(8,128)(2,1)S(1)}, u32[]{:S(2)}, u32[]{:S(2)}) collective-permute-start(bf16[16,2,512]{2,0,1:T(8,128)(2,1)S(1)} %maximum_select_fusion.14), channel_id=1, source_target_pairs={{0,8},{1,9},{2,10},{3,11},{4,12},{5,13},{6,14},{7,15},{8,0},{9,1},... | collective-permute-start | bytes 98312 | tf_op jit(solution)/shard_map/while/body/eval_jaxpr/ppermute | solution.py:22
  82.3 3.8 %collective-permute-start.4 = (bf16[16,512]{1,0:T(8,128)(2,1)S(1)}, bf16[16,512]{1,0:T(8,128)(2,1)S(1)}, u32[]{:S(2)}, u32[]{:S(2)}) collective-permute-start(bf16[16,512]{1,0:T(8,128)(2,1)S(1)} %fusion.98), channel_id=1, source_target_pairs={{16,0},{0,16},{17,1},{1,17},{18,2},{2,18},{19,3},{3,19},{20,4},{4,... | collective-permute-start | bytes 49160 | tf_op jit(solution)/shard_map/while/body/eval_jaxpr/ppermute | solution.py:33
  109.1 11.0 %collective-permute-start = (bf16[16,2,64]{2,0,1:T(8,128)(2,1)S(1)}, bf16[16,2,64]{2,0,1:T(8,128)(2,1)S(1)}, u32[]{:S(2)}, u32[]{:S(2)}) collective-permute-start(bf16[16,2,64]{2,0,1:T(8,128)(2,1)S(1)} %convolution_convert_fusion.2), channel_id=1, source_target_pairs={{0,1},{1,0},{2,3},{3,2},{4,5},{5,4},{6,7},{7,6},{8,9},{9,8},{10,11... | collective-permute-start | bytes 12296 | tf_op jit(solution)/shard_map/while/body/eval_jaxpr/ppermute | solution.py:22
  120.2 3.7 %collective-permute-start.1 = (bf16[16,2,128]{2,0,1:T(8,128)(2,1)S(1)}, bf16[16,2,128]{2,0,1:T(8,128)(2,1)S(1)}, u32[]{:S(2)}, u32[]{:S(2)}) collective-permute-start(bf16[16,2,128]{2,0,1:T(8,128)(2,1)S(1)} %maximum_select_fusion.12), channel_id=1, source_target_pairs={{0,2},{1,3},{2,0},{3,1},{4,6},{5,7},{6,4},{7,5},{8,10},{9,11},{10,... | collective-permute-start | bytes 24584 | tf_op jit(solution)/shard_map/while/body/eval_jaxpr/ppermute | solution.py:22
  123.9 3.7 %collective-permute-start.2 = (bf16[16,2,256]{2,0,1:T(8,128)(2,1)S(1)}, bf16[16,2,256]{2,0,1:T(8,128)(2,1)S(1)}, u32[]{:S(2)}, u32[]{:S(2)}) collective-permute-start(bf16[16,2,256]{2,0,1:T(8,128)(2,1)S(1)} %maximum_select_fusion.13), channel_id=1, source_target_pairs={{0,4},{1,5},{2,6},{3,7},{4,0},{5,1},{6,2},{7,3},{8,12},{9,13},{10,... | collective-permute-start | bytes 49160 | tf_op jit(solution)/shard_map/while/body/eval_jaxpr/ppermute | solution.py:22
  127.6 4.9 %collective-permute-start.3 = (bf16[16,2,512]{2,0,1:T(8,128)(2,1)S(1)}, bf16[16,2,512]{2,0,1:T(8,128)(2,1)S(1)}, u32[]{:S(2)}, u32[]{:S(2)}) collective-permute-start(bf16[16,2,512]{2,0,1:T(8,128)(2,1)S(1)} %maximum_select_fusion.14), channel_id=1, source_target_pairs={{0,8},{1,9},{2,10},{3,11},{4,12},{5,13},{6,14},{7,15},{8,0},{9,1},... | collective-permute-start | bytes 98312 | tf_op jit(solution)/shard_map/while/body/eval_jaxpr/ppermute | solution.py:22
  159.1 3.8 %collective-permute-start.4 = (bf16[16,512]{1,0:T(8,128)(2,1)S(1)}, bf16[16,512]{1,0:T(8,128)(2,1)S(1)}, u32[]{:S(2)}, u32[]{:S(2)}) collective-permute-start(bf16[16,512]{1,0:T(8,128)(2,1)S(1)} %fusion.98), channel_id=1, source_target_pairs={{16,0},{0,16},{17,1},{1,17},{18,2},{2,18},{19,3},{3,19},{20,4},{4,... | collective-permute-start | bytes 49160 | tf_op jit(solution)/shard_map/while/body/eval_jaxpr/ppermute | solution.py:33
  185.9 11.0 %collective-permute-start = (bf16[16,2,64]{2,0,1:T(8,128)(2,1)S(1)}, bf16[16,2,64]{2,0,1:T(8,128)(2,1)S(1)}, u32[]{:S(2)}, u32[]{:S(2)}) collective-permute-start(bf16[16,2,64]{2,0,1:T(8,128)(2,1)S(1)} %convolution_convert_fusion.2), channel_id=1, source_target_pairs={{0,1},{1,0},{2,3},{3,2},{4,5},{5,4},{6,7},{7,6},{8,9},{9,8},{10,11... | collective-permute-start | bytes 12296 | tf_op jit(solution)/shard_map/while/body/eval_jaxpr/ppermute | solution.py:22
  197.0 3.7 %collective-permute-start.1 = (bf16[16,2,128]{2,0,1:T(8,128)(2,1)S(1)}, bf16[16,2,128]{2,0,1:T(8,128)(2,1)S(1)}, u32[]{:S(2)}, u32[]{:S(2)}) collective-permute-start(bf16[16,2,128]{2,0,1:T(8,128)(2,1)S(1)} %maximum_select_fusion.12), channel_id=1, source_target_pairs={{0,2},{1,3},{2,0},{3,1},{4,6},{5,7},{6,4},{7,5},{8,10},{9,11},{10,... | collective-permute-start | bytes 24584 | tf_op jit(solution)/shard_map/while/body/eval_jaxpr/ppermute | solution.py:22
  200.7 3.7 %collective-permute-start.2 = (bf16[16,2,256]{2,0,1:T(8,128)(2,1)S(1)}, bf16[16,2,256]{2,0,1:T(8,128)(2,1)S(1)}, u32[]{:S(2)}, u32[]{:S(2)}) collective-permute-start(bf16[16,2,256]{2,0,1:T(8,128)(2,1)S(1)} %maximum_select_fusion.13), channel_id=1, source_target_pairs={{0,4},{1,5},{2,6},{3,7},{4,0},{5,1},{6,2},{7,3},{8,12},{9,13},{10,... | collective-permute-start | bytes 49160 | tf_op jit(solution)/shard_map/while/body/eval_jaxpr/ppermute | solution.py:22
  204.4 4.9 %collective-permute-start.3 = (bf16[16,2,512]{2,0,1:T(8,128)(2,1)S(1)}, bf16[16,2,512]{2,0,1:T(8,128)(2,1)S(1)}, u32[]{:S(2)}, u32[]{:S(2)}) collective-permute-start(bf16[16,2,512]{2,0,1:T(8,128)(2,1)S(1)} %maximum_select_fusion.14), channel_id=1, source_target_pairs={{0,8},{1,9},{2,10},{3,11},{4,12},{5,13},{6,14},{7,15},{8,0},{9,1},... | collective-permute-start | bytes 98312 | tf_op jit(solution)/shard_map/while/body/eval_jaxpr/ppermute | solution.py:22
  235.9 3.8 %collective-permute-start.4 = (bf16[16,512]{1,0:T(8,128)(2,1)S(1)}, bf16[16,512]{1,0:T(8,128)(2,1)S(1)}, u32[]{:S(2)}, u32[]{:S(2)}) collective-permute-start(bf16[16,512]{1,0:T(8,128)(2,1)S(1)} %fusion.98), channel_id=1, source_target_pairs={{16,0},{0,16},{17,1},{1,17},{18,2},{2,18},{19,3},{3,19},{20,4},{4,... | collective-permute-start | bytes 49160 | tf_op jit(solution)/shard_map/while/body/eval_jaxpr/ppermute | solution.py:33
  262.7 11.0 %collective-permute-start = (bf16[16,2,64]{2,0,1:T(8,128)(2,1)S(1)}, bf16[16,2,64]{2,0,1:T(8,128)(2,1)S(1)}, u32[]{:S(2)}, u32[]{:S(2)}) collective-permute-start(bf16[16,2,64]{2,0,1:T(8,128)(2,1)S(1)} %convolution_convert_fusion.2), channel_id=1, source_target_pairs={{0,1},{1,0},{2,3},{3,2},{4,5},{5,4},{6,7},{7,6},{8,9},{9,8},{10,11... | collective-permute-start | bytes 12296 | tf_op jit(solution)/shard_map/while/body/eval_jaxpr/ppermute | solution.py:22
  273.8 3.7 %collective-permute-start.1 = (bf16[16,2,128]{2,0,1:T(8,128)(2,1)S(1)}, bf16[16,2,128]{2,0,1:T(8,128)(2,1)S(1)}, u32[]{:S(2)}, u32[]{:S(2)}) collective-permute-start(bf16[16,2,128]{2,0,1:T(8,128)(2,1)S(1)} %maximum_select_fusion.12), channel_id=1, source_target_pairs={{0,2},{1,3},{2,0},{3,1},{4,6},{5,7},{6,4},{7,5},{8,10},{9,11},{10,... | collective-permute-start | bytes 24584 | tf_op jit(solution)/shard_map/while/body/eval_jaxpr/ppermute | solution.py:22
  277.4 3.7 %collective-permute-start.2 = (bf16[16,2,256]{2,0,1:T(8,128)(2,1)S(1)}, bf16[16,2,256]{2,0,1:T(8,128)(2,1)S(1)}, u32[]{:S(2)}, u32[]{:S(2)}) collective-permute-start(bf16[16,2,256]{2,0,1:T(8,128)(2,1)S(1)} %maximum_select_fusion.13), channel_id=1, source_target_pairs={{0,4},{1,5},{2,6},{3,7},{4,0},{5,1},{6,2},{7,3},{8,12},{9,13},{10,... | collective-permute-start | bytes 49160 | tf_op jit(solution)/shard_map/while/body/eval_jaxpr/ppermute | solution.py:22
  281.2 4.9 %collective-permute-start.3 = (bf16[16,2,512]{2,0,1:T(8,128)(2,1)S(1)}, bf16[16,2,512]{2,0,1:T(8,128)(2,1)S(1)}, u32[]{:S(2)}, u32[]{:S(2)}) collective-permute-start(bf16[16,2,512]{2,0,1:T(8,128)(2,1)S(1)} %maximum_select_fusion.14), channel_id=1, source_target_pairs={{0,8},{1,9},{2,10},{3,11},{4,12},{5,13},{6,14},{7,15},{8,0},{9,1},... | collective-permute-start | bytes 98312 | tf_op jit(solution)/shard_map/while/body/eval_jaxpr/ppermute | solution.py:22
  312.7 3.8 %collective-permute-start.4 = (bf16[16,512]{1,0:T(8,128)(2,1)S(1)}, bf16[16,512]{1,0:T(8,128)(2,1)S(1)}, u32[]{:S(2)}, u32[]{:S(2)}) collective-permute-start(bf16[16,512]{1,0:T(8,128)(2,1)S(1)} %fusion.98), channel_id=1, source_target_pairs={{16,0},{0,16},{17,1},{1,17},{18,2},{2,18},{19,3},{3,19},{20,4},{4,... | collective-permute-start | bytes 49160 | tf_op jit(solution)/shard_map/while/body/eval_jaxpr/ppermute | solution.py:33
  316.5 0.6 copy-start.4
